TPU v7x, 32 devices: a whole 2x2x4 slice. The times are simulated.
32 devices in a mesh: wide: 8 (over z, x), narrow: 4 (over y, core).
Axes of the slice: x: 2, y: 2, z: 4, core: 2. Of those that a mesh axis runs over, the one named last changes fastest.
Arguments:
- tokens: bfloat16 [36864, 768], P(('wide', 'narrow')), may hold values from -6 to 6
- ln1_gain: bfloat16 [768], replicated, may hold values from 0.25 to 1.75
- ln1_bias: bfloat16 [768], replicated, may hold values from -4 to 4
- w_qkv: bfloat16 [768, 2304], replicated, may hold values from -0.21875 to 0.21875
- b_qkv: bfloat16 [2304], replicated, may hold values from -4 to 4
- qnorm_gain: bfloat16 [64], replicated, may hold values from 0.25 to 1.75
- qnorm_bias: bfloat16 [64], replicated, may hold values from -4 to 4
- knorm_gain: bfloat16 [64], replicated, may hold values from 0.25 to 1.75
- w_out: bfloat16 [768, 768], replicated, may hold values from -0.875 to 0.875
- b_out: bfloat16 [768], replicated, may hold values from -4 to 4
- ln2_gain: bfloat16 [768], replicated, may hold values from 0.25 to 1.75
- ln2_bias: bfloat16 [768], replicated, may hold values from -4 to 4
- w_up: bfloat16 [768, 3072], replicated, may hold values from -0.21875 to 0.21875
- b_up: bfloat16 [3072], replicated, may hold values from -4 to 4
- w_down: bfloat16 [3072, 768], replicated, may hold values from -0.109375 to 0.109375
- b_down: bfloat16 [768], replicated, may hold values from -4 to 4
- segment_ids: int32 [36864], P(('wide', 'narrow')), may hold values from -1 to 15, as said below
- bucket_ids: int32 [8], P('wide'), may hold values from 0 to 1, as said below
- share_counts: int32 [2], replicated, may hold values from 1000 to 99999
- cotangent: bfloat16 [36864, 768], P(('wide', 'narrow')), may hold values from -6 to 6
Outputs:
- out_tokens: bfloat16 [36864, 768], P(('wide', 'narrow'))
- grad_tokens: bfloat16 [36864, 768], P(('wide', 'narrow'))
- grad_ln1_gain: float32 [768], replicated
- grad_ln1_bias: float32 [768], replicated
- grad_w_qkv: float32 [768, 2304], replicated
- grad_b_qkv: float32 [2304], replicated
- grad_qnorm_gain: float32 [64], replicated
- grad_qnorm_bias: float32 [64], replicated
- grad_knorm_gain: float32 [64], replicated
- grad_w_out: float32 [768, 768], replicated
- grad_b_out: float32 [768], replicated
- grad_ln2_gain: float32 [768], replicated
- grad_ln2_bias: float32 [768], replicated
- grad_w_up: float32 [768, 3072], replicated
- grad_b_up: float32 [3072], replicated
- grad_w_down: float32 [3072, 768], replicated
- grad_b_down: float32 [768], replicated
Inputs may be any that keep to these rules, and one draw needn't show every extreme that they name: bucket_ids is 1 on the indices of wide below a split and 0 on the rest; both buckets are present. `segment_ids`: within a device's block of 1152 slots, a large-bucket block holds 2 image slots of 576, a small-bucket block slots of 64; slot j's patches come first in it and carry the number j, the rest of the slot is -1; slot 0 is always full; in a small-bucket block the last eighth of the slots is empty.
All inputs are finite; a program needn't handle non-finite values.
Results may differ from a plain program's by a relative error of at most 0.012.
Values sent between devices are 32-bit elements; how exact they have to be, the bound alone decides.
A program may use at most 384 MiB of HBM per device.

v0:
```python
import jax
import jax.numpy as jnp
from jax import lax
from jax.sharding import PartitionSpec as P

EPS = 1e-06


def norm_rows(v):
    centred = v - jnp.mean(v, axis=-1, keepdims=True)
    return centred * lax.rsqrt(jnp.mean(centred * centred, axis=-1, keepdims=True) + EPS)


def norm_affine(v, gain, bias):
    return norm_rows(v) * gain + bias


def norm_scale(v, gain):
    return norm_rows(v) * gain


def gelu_exact(v):
    return jax.nn.gelu(v, approximate=False)


def outer(left, right):
    return lax.dot_general(
        left, right, (((0,), (0,)), ((), ())), preferred_element_type=jnp.float32
    )


def times_transpose(left, weight):
    return lax.dot_general(
        left, weight, (((1,), (1,)), ((), ())), preferred_element_type=jnp.float32
    )


def column_sums(grad16):
    return jnp.sum(grad16.astype(jnp.float32), axis=0)


def on_device(
    tokens,
    ln1_gain,
    ln1_bias,
    w_qkv,
    b_qkv,
    qnorm_gain,
    qnorm_bias,
    knorm_gain,
    w_out,
    b_out,
    ln2_gain,
    ln2_bias,
    w_up,
    b_up,
    w_down,
    b_down,
    segment_ids,
    bucket_ids,
    share_counts,
    cotangent,
):
    rows, width = tokens.shape
    head_dim = qnorm_gain.shape[0]
    heads = width // head_dim
    scale = head_dim ** (-0.5)
    g_one = ln1_gain.astype(jnp.float32)
    b_one = ln1_bias.astype(jnp.float32)
    q_gain = qnorm_gain.astype(jnp.float32)
    q_bias = qnorm_bias.astype(jnp.float32)
    k_gain = knorm_gain.astype(jnp.float32)
    g_two = ln2_gain.astype(jnp.float32)
    b_two = ln2_bias.astype(jnp.float32)
    inputs = tokens.astype(jnp.float32)
    normed1, ln1_back = jax.vjp(norm_affine, inputs, g_one, b_one)
    hidden1 = normed1.astype(jnp.bfloat16)
    project = jnp.dot(hidden1, w_qkv, preferred_element_type=jnp.float32) + b_qkv.astype(
        jnp.float32
    )
    queries = project[:, :width].reshape(rows, heads, head_dim)
    keys = project[:, width : 2 * width].reshape(rows, heads, head_dim)
    values = project[:, 2 * width :].reshape(rows, heads, head_dim)
    qnormed, qnorm_back = jax.vjp(norm_affine, queries, q_gain, q_bias)
    knormed, knorm_back = jax.vjp(norm_scale, keys, k_gain)
    query16 = qnormed.astype(jnp.bfloat16)
    key16 = knormed.astype(jnp.bfloat16)
    value16 = values.astype(jnp.bfloat16)
    blocks = max(1, rows // 512)
    block_rows = rows // blocks
    q_blocks = query16.reshape(blocks, block_rows, heads, head_dim)
    seg_blocks = segment_ids.reshape(blocks, block_rows)

    def scores_of(q_part, seg_part):
        scores = (
            jnp.einsum("qhd,khd->hqk", q_part, key16, preferred_element_type=jnp.float32) * scale
        )
        same = seg_part[:, None] == segment_ids[None, :]
        return jnp.where(same[None], scores, -1000000000.0)

    def forward_block(pieces):
        q_part, seg_part = pieces
        scores = scores_of(q_part, seg_part)
        top = jnp.max(scores, axis=-1, keepdims=True)
        expo = jnp.exp(scores - top)
        total = jnp.sum(expo, axis=-1, keepdims=True)
        probs = expo / total
        result = jnp.einsum(
            "hqk,khd->qhd", probs.astype(jnp.bfloat16), value16, preferred_element_type=jnp.float32
        )
        return (result, top[..., 0] + jnp.log(total[..., 0]))

    attended, log_sums = lax.map(forward_block, (q_blocks, seg_blocks))
    attended16 = attended.reshape(rows, width).astype(jnp.bfloat16)
    branch = jnp.dot(attended16, w_out, preferred_element_type=jnp.float32) + b_out.astype(
        jnp.float32
    )
    resid = inputs + branch
    normed2, ln2_back = jax.vjp(norm_affine, resid, g_two, b_two)
    hidden2 = normed2.astype(jnp.bfloat16)
    upper = jnp.dot(hidden2, w_up, preferred_element_type=jnp.float32) + b_up.astype(jnp.float32)
    act, gelu_back = jax.vjp(gelu_exact, upper)
    act16 = act.astype(jnp.bfloat16)
    mlp = jnp.dot(act16, w_down, preferred_element_type=jnp.float32) + b_down.astype(jnp.float32)
    out_tokens = (resid + mlp).astype(jnp.bfloat16)
    live = (segment_ids >= 0).astype(jnp.float32)
    grad_out = cotangent.astype(jnp.float32) * live[:, None]
    grad_mlp16 = grad_out.astype(jnp.bfloat16)
    d_w_down = outer(act16, grad_mlp16)
    d_b_down = column_sums(grad_mlp16)
    grad_act = times_transpose(grad_mlp16, w_down)
    (grad_upper,) = gelu_back(grad_act)
    grad_up16 = grad_upper.astype(jnp.bfloat16)
    d_w_up = outer(hidden2, grad_up16)
    d_b_up = column_sums(grad_up16)
    grad_hidden2 = times_transpose(grad_up16, w_up)
    grad_resid_norm, d_g_two, d_b_two = ln2_back(grad_hidden2)
    grad_resid = grad_out + grad_resid_norm
    grad_branch16 = grad_resid.astype(jnp.bfloat16)
    d_w_out = outer(attended16, grad_branch16)
    d_b_out = column_sums(grad_branch16)
    grad_att16 = times_transpose(grad_branch16, w_out).astype(jnp.bfloat16)
    grad_att_blocks = grad_att16.reshape(blocks, block_rows, heads, head_dim)

    def backward_block(carry, pieces):
        key_total, value_total = carry
        q_part, seg_part, lse_part, grad_part = pieces
        scores = scores_of(q_part, seg_part)
        probs = jnp.exp(scores - lse_part[..., None])
        grad_probs = jnp.einsum(
            "qhd,khd->hqk", grad_part, value16, preferred_element_type=jnp.float32
        )
        inner = jnp.sum(probs * grad_probs, axis=-1, keepdims=True)
        grad_scores16 = (probs * (grad_probs - inner)).astype(jnp.bfloat16)
        grad_query = (
            jnp.einsum("hqk,khd->qhd", grad_scores16, key16, preferred_element_type=jnp.float32)
            * scale
        )
        key_total = (
            key_total
            + jnp.einsum("hqk,qhd->khd", grad_scores16, q_part, preferred_element_type=jnp.float32)
            * scale
        )
        value_total = value_total + jnp.einsum(
            "hqk,qhd->khd",
            probs.astype(jnp.bfloat16),
            grad_part,
            preferred_element_type=jnp.float32,
        )
        return ((key_total, value_total), grad_query)

    zeros = jnp.zeros((rows, heads, head_dim), jnp.float32)
    (grad_knormed, grad_values), grad_q_blocks = lax.scan(
        backward_block, (zeros, zeros), (q_blocks, seg_blocks, log_sums, grad_att_blocks)
    )
    grad_queries, d_q_gain, d_q_bias = qnorm_back(grad_q_blocks.reshape(rows, heads, head_dim))
    grad_keys, d_k_gain = knorm_back(grad_knormed)
    grad_project16 = jnp.concatenate(
        [
            grad_queries.reshape(rows, width),
            grad_keys.reshape(rows, width),
            grad_values.reshape(rows, width),
        ],
        axis=1,
    ).astype(jnp.bfloat16)
    d_w_qkv = outer(hidden1, grad_project16)
    d_b_qkv = column_sums(grad_project16)
    grad_hidden1 = times_transpose(grad_project16, w_qkv)
    grad_in_norm, d_g_one, d_b_one = ln1_back(grad_hidden1)
    grad_tokens = (grad_resid + grad_in_norm).astype(jnp.bfloat16)
    counts = share_counts.astype(jnp.float32)
    share = jnp.sum(jnp.where(jnp.arange(2) == bucket_ids[0], counts, 0.0)) / jnp.sum(counts)
    total_slots = lax.axis_size("wide") * lax.axis_size("narrow") * rows
    factor = share * lax.rsqrt(jnp.float32(total_slots))
    local = (
        d_g_one * factor,
        d_b_one * factor,
        d_w_qkv * factor,
        d_b_qkv * factor,
        d_q_gain * factor,
        d_q_bias * factor,
        d_k_gain * factor,
        d_w_out * factor,
        d_b_out * factor,
        d_g_two * factor,
        d_b_two * factor,
        d_w_up * factor,
        d_b_up * factor,
        d_w_down * factor,
        d_b_down * factor,
    )
    summed = lax.psum(
        (
            local[0],
            local[1],
            local[2],
            local[3],
            local[4],
            local[5],
            local[6],
            local[7],
            local[8],
            local[9],
            local[10],
            local[11],
            local[12],
            local[13],
            local[14],
        ),
        ("wide", "narrow"),
    )
    return (
        out_tokens,
        grad_tokens,
        summed[0],
        summed[1],
        summed[2],
        summed[3],
        summed[4],
        summed[5],
        summed[6],
        summed[7],
        summed[8],
        summed[9],
        summed[10],
        summed[11],
        summed[12],
        summed[13],
        summed[14],
    )


def solution(mesh):
    in_specs = (
        P(("wide", "narrow"), None),
        P(),
        P(),
        P(),
        P(),
        P(),
        P(),
        P(),
        P(),
        P(),
        P(),
        P(),
        P(),
        P(),
        P(),
        P(),
        P(("wide", "narrow")),
        P("wide"),
        P(),
        P(("wide", "narrow"), None),
    )
    out_specs = (
        P(("wide", "narrow"), None),
        P(("wide", "narrow"), None),
        P(),
        P(),
        P(),
        P(),
        P(),
        P(),
        P(),
        P(),
        P(),
        P(),
        P(),
        P(),
        P(),
        P(),
        P(),
    )
    return jax.shard_map(
        on_device, mesh=mesh, in_specs=in_specs, out_specs=out_specs, check_vma=False
    )
```

profile of v0, /device:TPU:0, one launch (start us, length us, event | category | flops | bytes accessed | tf_op | source)
XLA Modules:
  0.0 1161.6 jit_solution(12897673866855606788)
XLA Ops:
  30.2 5.2 copy.58
  35.4 6.3 reshape.314
  69.1 5.2 copy.60
  91.3 101.7 %while.29 = (s32[]{:T(128)}, bf16[2,576,12,64]{1,3,2,0:T(8,128)(2,1)}, f32[2,12,576]{2,1,0:T(8,128)}, s32[2,576]{1,0:T(2,128)S(1)}, s32[1152]{0:T(1024)S(1)}, /*...) while((s32[]{:T(128)}, ...), condition=%wide.region_9.10_spmd.clone, body=%wide.region_6.9_spmd.sunk.clone | while | flops 2102789376 | bytes 103580040 | solution.py:113
  91.9 18.2 %fusion.129 = (f32[12,576]{1,0:T(8,128)S(1)}, f32[12,576,1152]{2,1,0:T(8,128)}) fusion(bf16[1152,12,64]{0,2,1:T(8,128)(2,1)} %get-tuple-element.520, bf16[2,576,12,64]{1,3,2,0:T(8,128)(2,1)} %get-tuple-element.519, s32[]{:T(128)S(6)} %copy.95, pred[576,1152]{1,0:T(8,128)(4,1)S(1)} %broadcast_compare_fusion.6), kind=kOutput, calls=%fused_computation.153.clone.1.clone | convolution fusion | flops 1043096832 | bytes 35294212 | tf_op jit(solution)/shard_map/while/body/eval_jaxpr/qhd,khd->hqk/dot_general | solution.py:96
  110.7 15.4 %fusion.130 = f32[12,576]{1,0:T(8,128)} fusion(f32[12,576,1152]{2,1,0:T(8,128)} %get-tuple-element.460, f32[12,576]{1,0:T(8,128)S(1)} %get-tuple-element.461), kind=kLoop, calls=%fused_computation.3.clone.1.clone | loop fusion | flops 15918336 | bytes 31905792 | tf_op jit(solution)/shard_map/while/body/eval_jaxpr/reduce_sum | solution.py:106
  126.1 14.5 %bitcast_dynamic-update-slice_fusion.9 = bf16[2,576,12,64]{1,3,2,0:T(8,128)(2,1)} fusion(bf16[2,576,12,64]{1,3,2,0:T(8,128)(2,1)} %get-tuple-element.507, s32[]{:T(128)S(6)} %copy.95, bf16[1152,12,64]{0,2,1:T(8,128)(2,1)} %get-tuple-element.521, f32[12,576,1152]{2,1,0:T(8,128)} %get-tuple-element.460, f32[12,576]{1,0:T(8,128)} %fusion.130, ...), kind=kOutput, calls=%fused_computation.5.clone.1.clone | convolution fusion | flops 1043103744 | bytes 35471364 | tf_op jit(solution)/shard_map/while/body/eval_jaxpr/hqk,khd->qhd/dot_general | solution.py:108
  142.5 18.2 %fusion.129 = (f32[12,576]{1,0:T(8,128)S(1)}, f32[12,576,1152]{2,1,0:T(8,128)}) fusion(bf16[1152,12,64]{0,2,1:T(8,128)(2,1)} %get-tuple-element.520, bf16[2,576,12,64]{1,3,2,0:T(8,128)(2,1)} %get-tuple-element.519, s32[]{:T(128)S(6)} %copy.95, pred[576,1152]{1,0:T(8,128)(4,1)S(1)} %broadcast_compare_fusion.6), kind=kOutput, calls=%fused_computation.153.clone.1.clone | convolution fusion | flops 1043096832 | bytes 35294212 | tf_op jit(solution)/shard_map/while/body/eval_jaxpr/qhd,khd->hqk/dot_general | solution.py:96
  161.3 15.4 %fusion.130 = f32[12,576]{1,0:T(8,128)} fusion(f32[12,576,1152]{2,1,0:T(8,128)} %get-tuple-element.460, f32[12,576]{1,0:T(8,128)S(1)} %get-tuple-element.461), kind=kLoop, calls=%fused_computation.3.clone.1.clone | loop fusion | flops 15918336 | bytes 31905792 | tf_op jit(solution)/shard_map/while/body/eval_jaxpr/reduce_sum | solution.py:106
  176.7 14.5 %bitcast_dynamic-update-slice_fusion.9 = bf16[2,576,12,64]{1,3,2,0:T(8,128)(2,1)} fusion(bf16[2,576,12,64]{1,3,2,0:T(8,128)(2,1)} %get-tuple-element.507, s32[]{:T(128)S(6)} %copy.95, bf16[1152,12,64]{0,2,1:T(8,128)(2,1)} %get-tuple-element.521, f32[12,576,1152]{2,1,0:T(8,128)} %get-tuple-element.460, f32[12,576]{1,0:T(8,128)} %fusion.130, ...), kind=kOutput, calls=%fused_computation.5.clone.1.clone | convolution fusion | flops 1043103744 | bytes 35471364 | tf_op jit(solution)/shard_map/while/body/eval_jaxpr/hqk,khd->qhd/dot_general | solution.py:108
  217.0 43.6 %multiply_convert_fusion.1 = (bf16[1152,3072]{1,0:T(8,128)(2,1)}, f32[1152,3072]{1,0:T(8,128)}, f32[1152,3072]{1,0:T(8,128)}) fusion(f32[3072]{0:T(1024)} %convert_element_type.128, bf16[768,3072]{1,0:T(8,128)(2,1)} %param.36, f32[1152,768]{0,1:T(8,128)} %copy-done.8, f32[768]{0:T(1024)} %convert_element_type.126, f32[768]{0:T(1024)} %convert_element_type.125, ...), kind=kOutput, calls=%fused_computation.43 | convolution fusion | flops 5673811968 | bytes 43674624 | tf_op jit(solution)/shard_map/dot_general | solution.py:121
  260.6 20.7 %convert_reduce_fusion = (f32[3072]{0:T(1024)}, bf16[1152,3072]{1,0:T(8,128)(2,1)}) fusion(f32[1152,3072]{1,0:T(8,128)} %get-tuple-element.300, f32[1152,3072]{1,0:T(8,128)} %get-tuple-element.312, bf16[3072,768]{1,0:T(8,128)(2,1)} %param.38, bf16[1152,768]{0,1:T(8,128)(2,1)} %copy.65, f32[1152]{0:T(1024)} %compare_convert_fusion), kind=kOutput, calls=%fused_computation.41 | convolution fusion | flops 5495092224 | bytes 41894400 | tf_op jit(solution)/shard_map/dot_general | solution.py:33
  281.3 11.2 fusion.71
  292.5 5.2 copy.66
  313.7 5.4 reshape.317
  322.4 222.0 %while.30 = (s32[]{:T(128)}, f32[1152,12,64]{0,2,1:T(8,128)}, f32[1152,12,64]{0,2,1:T(8,128)}, f32[2,576,12,64]{1,3,2,0:T(8,128)}, bf16[2,576,12,64]{1,3,2,0:T(8...) while((s32[]{:T(128)}, f32[1152,12,64]{0,2,1:T(8,128)}, ...), condition=%wide.region_16.17_spmd.clone.clone, body=%wide.region_14.16_spmd.clone.sunk.clone | while | flops 5173265408 | bytes 265952688 | solution.py:173
  322.8 16.6 %fusion.140 = f32[12,576,1152]{2,1,0:T(8,128)} fusion(bf16[1152,12,64]{0,2,1:T(8,128)(2,1)} %get-tuple-element.554, bf16[2,576,12,64]{1,3,2,0:T(8,128)(2,1)} %get-tuple-element.553, s32[]{:T(128)S(6)} %copy.105), kind=kOutput, calls=%fused_computation.25.clone.1.clone | convolution fusion | flops 1019215872 | bytes 34603012 | tf_op jit(solution)/shard_map/while/body/eval_jaxpr/qhd,khd->hqk/dot_general | solution.py:150
  341.3 30.0 %multiply_reduce_fusion.12 = (f32[12,576]{1,0:T(8,128)}, f32[12,576,1152]{2,1,0:T(8,128)}) fusion(f32[12,576,1152]{2,1,0:T(8,128)} %fusion.140, f32[12,576]{1,0:T(8,128)} %dynamic-slice_bitcast_fusion.3, bf16[1152,12,64]{0,2,1:T(8,128)(2,1)} %get-tuple-element.551, bf16[2,576,12,64]{1,3,2,0:T(8,128)(2,1)} %get-tuple-element.548, ...), kind=kOutput, calls=%fused_computation.13.clone.1.clone | convolution fusion | flops 1059022080 | bytes 67185664 | tf_op jit(solution)/shard_map/while/body/eval_jaxpr/qhd,khd->hqk/dot_general | solution.py:96
  371.3 26.3 %multiply_convert_fusion.5 = bf16[12,576,1152]{2,1,0:T(8,128)(2,1)} fusion(f32[12,576,1152]{2,1,0:T(8,128)} %get-tuple-element.483, f32[12,576,1152]{2,1,0:T(8,128)} %fusion.140, f32[12,576]{1,0:T(8,128)} %get-tuple-element.484), kind=kLoop, calls=%fused_computation.12.clone.1.clone | loop fusion | flops 23887872 | bytes 79653888 | tf_op jit(solution)/shard_map/while/body/eval_jaxpr/convert_element_type | solution.py:154
  397.5 10.6 fusion.141
  408.1 15.0 %fusion.142 = f32[1152,12,64]{0,2,1:T(8,128)} fusion(f32[12,576,1152]{2,1,0:T(8,128)} %get-tuple-element.483, f32[1152,12,64]{0,2,1:T(8,128)} %get-tuple-element.535, pred[]{:T(512)S(6)} %compare.4, bf16[2,576,12,64]{1,3,2,0:T(8,128)(2,1)} %get-tuple-element.553, s32[]{:T(128)S(6)} %copy.105), kind=kOutput, calls=%fused_computation.21.clone.1.clone | convolution fusion | flops 1028947968 | bytes 39911428 | tf_op jit(solution)/shard_map/while/body/eval_jaxpr/hqk,qhd->khd/dot_general | solution.py:164
  423.1 9.4 bitcast_dynamic-update-slice_fusion.11
  432.4 16.6 %fusion.140 = f32[12,576,1152]{2,1,0:T(8,128)} fusion(bf16[1152,12,64]{0,2,1:T(8,128)(2,1)} %get-tuple-element.554, bf16[2,576,12,64]{1,3,2,0:T(8,128)(2,1)} %get-tuple-element.553, s32[]{:T(128)S(6)} %copy.105), kind=kOutput, calls=%fused_computation.25.clone.1.clone | convolution fusion | flops 1019215872 | bytes 34603012 | tf_op jit(solution)/shard_map/while/body/eval_jaxpr/qhd,khd->hqk/dot_general | solution.py:150
  451.0 29.9 %multiply_reduce_fusion.12 = (f32[12,576]{1,0:T(8,128)}, f32[12,576,1152]{2,1,0:T(8,128)}) fusion(f32[12,576,1152]{2,1,0:T(8,128)} %fusion.140, f32[12,576]{1,0:T(8,128)} %dynamic-slice_bitcast_fusion.3, bf16[1152,12,64]{0,2,1:T(8,128)(2,1)} %get-tuple-element.551, bf16[2,576,12,64]{1,3,2,0:T(8,128)(2,1)} %get-tuple-element.548, ...), kind=kOutput, calls=%fused_computation.13.clone.1.clone | convolution fusion | flops 1059022080 | bytes 67185664 | tf_op jit(solution)/shard_map/while/body/eval_jaxpr/qhd,khd->hqk/dot_general | solution.py:96
  480.9 26.3 %multiply_convert_fusion.5 = bf16[12,576,1152]{2,1,0:T(8,128)(2,1)} fusion(f32[12,576,1152]{2,1,0:T(8,128)} %get-tuple-element.483, f32[12,576,1152]{2,1,0:T(8,128)} %fusion.140, f32[12,576]{1,0:T(8,128)} %get-tuple-element.484), kind=kLoop, calls=%fused_computation.12.clone.1.clone | loop fusion | flops 23887872 | bytes 79653888 | tf_op jit(solution)/shard_map/while/body/eval_jaxpr/convert_element_type | solution.py:154
  507.2 11.6 fusion.141
  518.8 16.0 %fusion.142 = f32[1152,12,64]{0,2,1:T(8,128)} fusion(f32[12,576,1152]{2,1,0:T(8,128)} %get-tuple-element.483, f32[1152,12,64]{0,2,1:T(8,128)} %get-tuple-element.535, pred[]{:T(512)S(6)} %compare.4, bf16[2,576,12,64]{1,3,2,0:T(8,128)(2,1)} %get-tuple-element.553, s32[]{:T(128)S(6)} %copy.105), kind=kOutput, calls=%fused_computation.21.clone.1.clone | convolution fusion | flops 1028947968 | bytes 39911428 | tf_op jit(solution)/shard_map/while/body/eval_jaxpr/hqk,qhd->khd/dot_general | solution.py:164
  534.8 9.4 bitcast_dynamic-update-slice_fusion.11
  544.3 7.1 copy.70
  551.4 5.5 reshape.319
  564.6 5.5 reshape.318
  572.8 5.3 convolution_multiply_fusion.4
  578.1 12.2 %convolution_multiply_fusion.3 = f32[768,3072]{1,0:T(8,128)} fusion(bf16[1152,3072]{1,0:T(8,128)(2,1)} %get-tuple-element.318, f32[]{:T(128)S(6)} %mul.458, f32[1152,768]{0,1:T(8,128)S(1)} %copy-done.10, f32[768]{0:T(1024)S(1)} %copy-done.63, f32[768]{0:T(1024)S(1)} %copy-done.52, f32[1152]{0:T(1024)S(1)} %copy-done.36, f32[1152]{0:T(1024)S(1)} %copy-done.34), kind=kOutput, calls=%fused_computation.63 | convolution fusion | flops 5442600960 | bytes 20069380 | tf_op jit(solution)/shard_map/dot_general | solution.py:27
  610.5 13.6 %multiply_reduce_fusion.1 = (f32[64]{0:T(128)}, f32[2,576,12]{1,0,2:T(2,128)S(1)}) fusion(f32[2,576,12,64]{1,0,3,2:T(2,128)} %reshape.314, f32[2,576,12]{1,0,2:T(2,128)} %copy-done.27, f32[2,576,12]{1,0,2:T(2,128)} %div.95, f32[2,576,12,64]{1,3,2,0:T(8,128)} %get-tuple-element.121, f32[2,576,12]{1,0,2:T(2,128)S(1)} %multiply_multiply_fusion.7, ...), kind=kLoop, calls=%fused_computation.79 | loop fusion | flops 8833472 | bytes 7299584 | tf_op jit(solution)/shard_map/transpose(jvp())/reduce_sum | solution.py:15
  629.2 5.2 copy.77
  637.3 5.2 copy.75
  645.4 5.2 copy.73
  653.5 5.2 copy.72
  665.1 11.7 %convolution_multiply_fusion.2 = f32[3072,768]{1,0:T(8,128)} fusion(bf16[1152,3072]{1,0:T(8,128)(2,1)} %get-tuple-element.299, f32[]{:T(128)S(6)} %mul.458, bf16[1152,768]{0,1:T(8,128)(2,1)} %copy.65, f32[1152]{0:T(1024)S(1)} %copy-done.44), kind=kOutput, calls=%fused_computation.62 | convolution fusion | flops 5440831488 | bytes 18289156 | tf_op jit(solution)/shard_map/dot_general | solution.py:27
  676.9 9.9 fusion.48
  686.8 10.5 convolution_multiply_fusion.1
  701.0 11.9 %fusion.50 = bf16[1152,768]{0,1:T(8,128)(2,1)} fusion(f32[1152,768]{0,1:T(8,128)} %copy-done.8, bf16[1152,3072]{1,0:T(8,128)(2,1)} %get-tuple-element.299, bf16[3072,768]{1,0:T(8,128)(2,1)} %param.38, f32[768]{0:T(1024)S(1)} %convert_element_type.130), kind=kOutput, calls=%fused_computation.109 | convolution fusion | flops 5438472192 | bytes 17107968 | tf_op jit(solution)/shard_map/dot_general | solution.py:124
  716.8 9.3 fusion.70
  726.1 5.2 copy.80
  754.7 45.8 %all-reduce = (f32[768]{0:T(1024)}, f32[768]{0:T(1024)}, f32[2304]{0:T(1024)}, f32[64]{0:T(128)}, f32[64]{0:T(128)}, /*index=5*/f32[64]{0:T(128)}, f32[768]{0:T(...) all-reduce(f32[768]{0:T(1024)} %get-tuple-element.324, ...), channel_id=1, replica_groups=mesh['wide'=8,'narrow'=4] {'wide','narrow'}, use_global_device_ids=true, to_apply=%region_26.27 | all-reduce | flops 10176 | bytes 81408 | tf_op jit(solution)/shard_map/psum | solution.py:212
  800.5 333.0 %all-reduce.4.cloned.1.call-done = (f32[768,2304]{1,0:T(8,128)}, f32[768,768]{1,0:T(8,128)}, f32[768,3072]{1,0:T(8,128)}, f32[3072,768]{1,0:T(8,128)}) async-done(((f32[768,2304]{1,0:T(8,128)}, f32[768,768]{1,0:T(8,128)}, f32[768,3072]{1,0:T(8,128)}, f32[3072,768]{1,0:T(8,128)}), (f32[768,2304]{1,0:T(8,128)}, f32[768,768]{1,0:T(8,128)}, f32[768,3072]{1,0:T(8,128)}, ...) | async-done | bytes 28311568 | tf_op jit(solution)/shard_map/psum | solution.py:212
  1133.5 6.6 copy.120
  1141.5 9.3 copy.122
  (257 shorter events, 203.9 us)
Async XLA Ops:
  7.2 12.2 %copy-start = (bf16[768,2304]{1,0:T(8,128)(2,1)S(1)}, bf16[768,2304]{1,0:T(8,128)(2,1)}, u32[]{:S(2)}) copy-start(bf16[768,2304]{1,0:T(8,128)(2,1)} %param.27) | copy-start | bytes 10616836
  7.2 6.3 copy-start.65
  7.2 1126.3 %all-reduce.4.cloned.1.call-start = ((), (), s32[]{:S(2)}) async-start(), calls=%async_computation | async-start | bytes 56623104 | tf_op jit(solution)/shard_map/psum | solution.py:212
  13.5 5.8 copy-start.4
  13.5 5.2 copy-start.61
  24.1 6.1 copy-start.16
  46.2 8.1 copy-start.23
  62.5 6.6 copy-start.27
  193.0 9.8 copy-start.31
  193.0 9.8 copy-start.59
  210.3 92.1 %copy-start.33 = (f32[1152]{0:T(1024)}, f32[1152]{0:T(1024)S(1)}, u32[]{:S(2)}) copy-start(f32[1152]{0:T(1024)S(1)} %broadcast_multiply_fusion.4) | copy-start | bytes 13828
  213.1 89.4 %copy-start.35 = (f32[1152]{0:T(1024)}, f32[1152]{0:T(1024)S(1)}, u32[]{:S(2)}) copy-start(f32[1152]{0:T(1024)S(1)} %fusion.57) | copy-start | bytes 13828
  297.7 4.8 copy-start.9
  297.7 5.2 copy-start.13
  297.7 5.2 copy-start.51
  313.7 8.6 copy-start.24
  313.7 8.6 copy-start.32
  322.8 16.6 %copy-start.28 = (f32[2,12,576]{2,1,0:T(8,128)S(1)}, f32[2,12,576]{2,1,0:T(8,128)}, u32[]{:S(2)}) copy-start(f32[2,12,576]{2,1,0:T(8,128)} %get-tuple-element.552) | copy-start | bytes 165892 | tf_op jit(solution)/shard_map/while
  432.4 16.6 %copy-start.28 = (f32[2,12,576]{2,1,0:T(8,128)S(1)}, f32[2,12,576]{2,1,0:T(8,128)}, u32[]{:S(2)}) copy-start(f32[2,12,576]{2,1,0:T(8,128)} %get-tuple-element.552) | copy-start | bytes 165892 | tf_op jit(solution)/shard_map/while
  551.4 5.5 copy-start.60
  564.6 6.2 copy-start.66
  572.7 5.3 copy-start.10
  572.8 5.3 copy-start.34
  572.8 5.3 copy-start.36
  572.8 5.3 copy-start.52
  572.8 5.3 copy-start.63
  578.1 12.2 %copy-start.3 = (f32[1152,12,64]{0,2,1:T(8,128)S(1)}, f32[1152,12,64]{0,2,1:T(8,128)}, u32[]{:S(2)}) copy-start(f32[1152,12,64]{0,2,1:T(8,128)} %get-tuple-element.123) | copy-start | bytes 10616836
  590.3 5.5 copy-start.58
  595.8 5.1 copy-start.1
  595.8 5.2 copy-start.2
  595.8 5.2 copy-start.19
  595.8 5.1 copy-start.25
  658.6 6.5 copy-start.44
  665.1 11.7 %copy-start.54 = (f32[768]{0:T(1024)S(1)}, f32[768]{0:T(1024)}, u32[]{:S(2)}) copy-start(f32[768]{0:T(1024)} %mul.428) | copy-start | bytes 9220
  676.9 9.9 copy-start.5
  676.9 9.9 copy-start.30
  676.9 9.9 copy-start.42
  676.9 9.9 copy-start.49
  676.9 9.9 copy-start.62
  740.5 5.1 copy-start.64
  740.5 7.6 copy-start.55
  740.5 7.6 copy-start.56
  740.5 8.2 copy-start.53
  744.5 9.6 copy-start.57
  1133.5 6.6 copy-start.20
  1140.0 10.7 slice-start
  1141.5 9.3 slice-start.1
  1141.5 9.3 slice-start.2
  (26 other events, 56.2 us)
Sparse Core Ops, SparseCore 0:
  697.5 435.9 all-reduce.3
where the time goes:
time: 1170 us; the launch traced here: 1160 us
  matrix products  379 us (32%)
  waiting for transfers between devices  333 us (28%)
  other arithmetic  202 us (17%)
  local copies, waits for them, and re-layouts  184 us (16%)
  blocking collectives  45.8 us (4%)
  between operations  16.8 us (1%)
    psum x1, waiting for transfers between devices, on_device(): lax.psum((local[0], local[1], local[2], local[3], local[4], local[5], loc...  333 us
    dot_general x4, matrix products, scores_of(): jnp.einsum('qhd,khd->hqk', q_part, key16, preferred_element_type=jnp.floa...  96.3 us
    convert_element_type x2, other arithmetic, backward_block(): grad_scores16 = (probs * (grad_probs - inner)).astype(jnp.bfloat16)  52.5 us
    unnamed x147, local copies, waits for them, and re-layouts  50.9 us
    psum x1, blocking collectives, on_device(): lax.psum((local[0], local[1], local[2], local[3], local[4], local[5], loc...  45.8 us
    dot_general x4, matrix products, times_transpose(): lax.dot_general(left, weight, (((1,), (1,)), ((), ())), preferred_element...  44 us
    dot_general x1, matrix products, on_device(): jnp.dot(hidden2, w_up, preferred_element_type=jnp.float32)  43.6 us
    dot_general x4, matrix products, outer(): lax.dot_general(left, right, (((0,), (0,)), ((), ())), preferred_element_...  39.7 us
  transfers between devices with their start and end apart: 1, of which 1 were waited for; matrix products, arithmetic and copies ran while one was open for 5% of the time, Pallas kernels for 0%

commit v1 on v0

v1 whole, which is shorter than its diff:
```python
import functools
import math

import jax
import jax.numpy as jnp
from jax import lax
from jax.experimental import pallas as pl
from jax.experimental.pallas import tpu as pltpu
from jax.sharding import PartitionSpec as P

EPS = 1e-06
F32 = jnp.float32
BF16 = jnp.bfloat16
NN = (((1,), (0,)), ((), ()))
NT = (((1,), (1,)), ((), ()))
MASKED = -1000000000.0
OPEN = 3.0e38
GROUP = 256
VMEM = 60 * 1024 * 1024


def dot(left, right, dims=NN):
    return lax.dot_general(left, right, dims, preferred_element_type=F32)


def row_stats(v):
    mean = jnp.mean(v, axis=-1, keepdims=True)
    centred = v - mean
    rstd = lax.rsqrt(jnp.mean(centred * centred, axis=-1, keepdims=True) + EPS)
    return centred * rstd, rstd


def head_mean(v, averager):
    high = v.astype(BF16)
    low = (v - high.astype(F32)).astype(BF16)
    return dot(high, averager) + dot(low, averager)


def averager_of(width, head_dim):
    row = lax.broadcasted_iota(jnp.int32, (width, width), 0) // head_dim
    col = lax.broadcasted_iota(jnp.int32, (width, width), 1) // head_dim
    return jnp.where(row == col, 1.0 / head_dim, 0.0).astype(BF16)


def row_loop(rows, chunk, body):
    def step(i, carry):
        body(pl.ds(pl.multiple_of(i * chunk, chunk), chunk))
        return carry

    lax.fori_loop(0, rows // chunk, step, 0)


def forward_kernel(
    head_dim,
    blocks,
    bucket_ref,
    x_ref,
    g1_ref,
    b1_ref,
    wq_ref,
    wk_ref,
    wv_ref,
    bq_ref,
    bk_ref,
    bv_ref,
    qg_ref,
    qb_ref,
    kg_ref,
    wo_ref,
    bo_ref,
    g2_ref,
    b2_ref,
    segc_ref,
    segr_ref,
    h1_ref,
    qn_ref,
    kn_ref,
    v_ref,
    qhat_ref,
    khat_ref,
    qrstd_ref,
    krstd_ref,
    lse_ref,
    ot_ref,
    r_ref,
    h2_ref,
    mask_s,
    vt_s,
    ot_s,
    o_s,
):
    rows, width = x_ref.shape
    group = wq_ref.shape[1]
    heads = group // head_dim
    span = rows // blocks
    chunk = span // 2
    step = pl.program_id(0)
    last = pl.num_programs(0) - 1
    scale = head_dim**-0.5

    @pl.when(step == 0)
    def _():
        def norm(at):
            hat, _ = row_stats(x_ref[at, :].astype(F32))
            h1_ref[at, :] = (hat * g1_ref[...] + b1_ref[...]).astype(BF16)

        row_loop(rows, span // 4, norm)
        for kb in range(blocks):
            for qb in range(blocks):
                same = segc_ref[kb * span : (kb + 1) * span, :] == segr_ref[qb]
                mask_s[kb, qb] = jnp.where(same, OPEN, MASKED)

    averager = averager_of(group, head_dim)

    def project(at):
        h1 = h1_ref[at, :]

        def normed(w_ref, bias_ref, hat_ref, rstd_ref):
            raw = dot(h1, w_ref[...]) + bias_ref[...]
            centred = raw - head_mean(raw, averager)
            rstd = lax.rsqrt(head_mean(centred * centred, averager) + EPS)
            hat = centred * rstd
            hat_ref[at, :] = hat
            rstd_ref[at, :] = rstd
            return hat

        qhat = normed(wq_ref, bq_ref, qhat_ref, qrstd_ref)
        qn_ref[at, :] = (qhat * qg_ref[...] + qb_ref[...]).astype(BF16)
        khat = normed(wk_ref, bk_ref, khat_ref, krstd_ref)
        kn_ref[at, :] = (khat * kg_ref[...]).astype(BF16)
        v_ref[at, :] = (dot(h1, wv_ref[...]) + bv_ref[...]).astype(BF16)

    row_loop(rows, chunk, project)
    for b in range(blocks):
        vt_s[b] = v_ref[b * span : (b + 1) * span, :].astype(F32).T.astype(BF16)

    lane_head = lax.broadcasted_iota(jnp.int32, (span, group), 1) // head_dim

    def attend(i, key_blocks):
        h = i // blocks
        qb = i % blocks
        queries = qn_ref[pl.ds(pl.multiple_of(qb * span, span), span), :]
        scores = []
        for kb in key_blocks(qb):
            keys = kn_ref[pl.ds(pl.multiple_of(kb * span, span), span), :] * jnp.asarray(scale, BF16)
            keys = jnp.where(lane_head == h, keys, jnp.zeros_like(keys))
            scores.append(jnp.minimum(dot(keys, queries, NT), mask_s[kb, qb]))
        top = functools.reduce(jnp.maximum, [jnp.max(s, axis=0, keepdims=True) for s in scores])
        expos = [jnp.exp(s - top) for s in scores]
        total = sum(jnp.sum(e, axis=0, keepdims=True) for e in expos)
        at = pl.ds(pl.multiple_of(h * head_dim, head_dim), head_dim)
        out = sum(
            dot(vt_s[kb, at, :], e.astype(BF16)) for kb, e in zip(key_blocks(qb), expos)
        )
        ot_s[qb, at, :] = out * (1.0 / total)
        lse_ref[h, qb] = top + jnp.log(total)

    large = bucket_ref[0] == 1

    @pl.when(large)
    def _():
        lax.fori_loop(
            0, heads * blocks, lambda i, c: (attend(i, lambda qb: [qb]), c)[1], 0
        )

    @pl.when(jnp.logical_not(large))
    def _():
        lax.fori_loop(
            0, heads * blocks, lambda i, c: (attend(i, lambda qb: list(range(blocks))), c)[1], 0
        )

    for b in range(blocks):
        piece = ot_s[b]
        ot_ref[b] = piece.astype(BF16)
        o_s[b * span : (b + 1) * span, :] = piece.T.astype(BF16)

    def out_project(at):
        part = dot(o_s[at, :], wo_ref[...])

        @pl.when(step == 0)
        def _():
            r_ref[at, :] = x_ref[at, :].astype(F32) + bo_ref[...] + part

        @pl.when(step > 0)
        def _():
            r_ref[at, :] += part

        @pl.when(step == last)
        def _():
            hat, _ = row_stats(r_ref[at, :])
            h2_ref[at, :] = (hat * g2_ref[...] + b2_ref[...]).astype(BF16)

    row_loop(rows, chunk, out_project)


def gelu_parts(u):
    size = jnp.abs(u) * (2.0**-0.5)
    below = 1.0 + 0.3275911 * size
    t = pl.reciprocal(below, approx=True)
    t = t * (2.0 - below * t)
    bell = jnp.exp(-0.5 * u * u)
    poly = t * (
        0.127414796
        + t * (-0.142248368 + t * (0.7107068705 + t * (-0.7265760135 + t * 0.5307027145)))
    )
    tail = poly * bell
    phi = jnp.where(u < 0.0, tail, 1.0 - tail)
    return phi, bell * (1.0 / math.sqrt(2.0 * math.pi))


def mlp_kernel(
    blocks,
    factor_ref,
    h2_ref,
    r_ref,
    cot_ref,
    live_ref,
    wu_ref,
    bu_ref,
    wd_ref,
    bd_ref,
    g2_ref,
    wo_ref,
    ot_ref,
    out_ref,
    gr_ref,
    go_ref,
    dwd_ref,
    dwu_ref,
    dwo_ref,
    dbu_ref,
    small_ref,
    gm_s,
    h2t_s,
    a_s,
    gu_s,
    m_s,
    gh2_s,
):
    rows, width = h2_ref.shape
    span = rows // blocks
    chunk = span // 2
    step = pl.program_id(0)
    last = pl.num_programs(0) - 1
    factor = factor_ref[0]

    @pl.when(step == 0)
    def _():
        small_ref[...] = jnp.zeros_like(small_ref)

        def start(at):
            gm = cot_ref[at, :].astype(F32) * live_ref[at, :]
            gm_s[at, :] = gm.astype(BF16)
            small_ref[0:1, :] += factor * jnp.sum(gm, axis=0, keepdims=True)
            m_s[at, :] = r_ref[at, :] + bd_ref[...]
            gh2_s[at, :] = jnp.zeros((chunk, width), F32)

        row_loop(rows, chunk, start)
        for i in range(rows // 128):
            h2t_s[:, i * 128 : (i + 1) * 128] = (
                h2_ref[i * 128 : (i + 1) * 128, :].astype(F32).T.astype(BF16)
            )

    dbu_ref[...] = jnp.zeros_like(dbu_ref)

    def middle(at):
        u = dot(h2_ref[at, :], wu_ref[...]) + bu_ref[...]
        phi, bell = gelu_parts(u)
        a = (u * phi).astype(BF16)
        a_s[at, :] = a
        ga = dot(gm_s[at, :], wd_ref[...], NT)
        gu = (ga * (phi + u * bell)).astype(BF16)
        gu_s[at, :] = gu
        dbu_ref[...] += factor * jnp.sum(gu.astype(F32), axis=0, keepdims=True)
        m_s[at, :] += dot(a, wd_ref[...])
        gh2_s[at, :] += dot(gu, wu_ref[...], NT)

    row_loop(rows, chunk // 2, middle)
    dwd_ref[...] = factor * lax.dot_general(
        a_s[...], gm_s[...], (((0,), (0,)), ((), ())), preferred_element_type=F32
    )
    dwu_ref[...] = factor * dot(h2t_s[...], gu_s[...])

    @pl.when(step == last)
    def _():
        def finish(at):
            out_ref[at, :] = m_s[at, :].astype(BF16)
            hat, rstd = row_stats(r_ref[at, :])
            gy = gh2_s[at, :]
            small_ref[1:2, :] += factor * jnp.sum(gy * hat, axis=0, keepdims=True)
            small_ref[2:3, :] += factor * jnp.sum(gy, axis=0, keepdims=True)
            gy = gy * g2_ref[...]
            first = jnp.mean(gy, axis=-1, keepdims=True)
            second = jnp.mean(gy * hat, axis=-1, keepdims=True)
            gr = gm_s[at, :].astype(F32) + rstd * (gy - first - hat * second)
            gr_ref[at, :] = gr
            gz = gr.astype(BF16)
            gm_s[at, :] = gz
            small_ref[3:4, :] += factor * jnp.sum(gz.astype(F32), axis=0, keepdims=True)
            go_ref[at, :] = dot(gz, wo_ref[...], NT).astype(BF16)

        row_loop(rows, chunk // 2, finish)
        dwo_ref[...] = factor * sum(
            dot(ot_ref[b], gm_s[b * span : (b + 1) * span, :]) for b in range(blocks)
        )


def backward_kernel(
    head_dim,
    blocks,
    factor_ref,
    x_ref,
    h1_ref,
    gr_ref,
    g1_ref,
    qg_ref,
    kg_ref,
    segc_ref,
    segr_ref,
    qn_ref,
    kn_ref,
    v_ref,
    go_ref,
    qhat_ref,
    khat_ref,
    qrstd_ref,
    krstd_ref,
    lse_ref,
    wq_ref,
    wk_ref,
    wv_ref,
    gx_ref,
    dw_ref,
    db_ref,
    small_ref,
    norm_ref,
    mask_s,
    h1t_s,
    kt_s,
    gqt_s,
    gq_s,
    gk_s,
    gv_s,
    g16_s,
    gh1_s,
):
    rows, width = x_ref.shape
    group = wq_ref.shape[1]
    heads = group // head_dim
    span = rows // blocks
    chunk = span // 2
    step = pl.program_id(0)
    last = pl.num_programs(0) - 1
    scale = jnp.asarray(head_dim**-0.5, BF16)
    factor = factor_ref[0]

    @pl.when(step == 0)
    def _():
        small_ref[...] = jnp.zeros_like(small_ref)
        norm_ref[...] = jnp.zeros_like(norm_ref)
        for b in range(blocks):
            same = segc_ref[b * span : (b + 1) * span, :] == segr_ref[b]
            mask_s[b] = jnp.where(same, OPEN, MASKED)
        for i in range(rows // 128):
            h1t_s[:, i * 128 : (i + 1) * 128] = (
                h1_ref[i * 128 : (i + 1) * 128, :].astype(F32).T.astype(BF16)
            )

        def zero(at):
            gh1_s[at, :] = jnp.zeros((chunk, width), F32)

        row_loop(rows, chunk, zero)

    def clear(at):
        gk_s[at, :] = jnp.zeros((chunk, group), F32)
        gv_s[at, :] = jnp.zeros((chunk, group), F32)

    row_loop(rows, chunk, clear)
    for b in range(blocks):
        kt_s[b] = (kn_ref[b * span : (b + 1) * span, :] * scale).astype(F32).T.astype(BF16)

    lane_head = lax.broadcasted_iota(jnp.int32, (span, group), 1) // head_dim

    def one(i, carry):
        h = i // blocks
        b = i % blocks
        at = pl.ds(pl.multiple_of(b * span, span), span)
        mine = lane_head == h

        def only(piece):
            return jnp.where(mine, piece, jnp.zeros_like(piece))

        queries = only(qn_ref[at, :] * scale)
        grads = only(go_ref[at, :])
        scores = jnp.minimum(dot(kn_ref[at, :], queries, NT), mask_s[b])
        probs = jnp.exp(scores - lse_ref[h, b])
        gprobs = dot(v_ref[at, :], grads, NT)
        inner = jnp.sum(probs * gprobs, axis=0, keepdims=True)
        gscores = (probs * (gprobs - inner)).astype(BF16)
        gv_s[at, :] += dot(probs.astype(BF16), grads)
        gk_s[at, :] += dot(gscores, queries)
        lanes = pl.ds(pl.multiple_of(h * head_dim, head_dim), head_dim)
        gqt_s[b, lanes, :] = dot(kt_s[b, lanes, :], gscores)
        return carry

    lax.fori_loop(0, heads * blocks, one, 0)
    for b in range(blocks):
        gq_s[b * span : (b + 1) * span, :] = gqt_s[b].T

    averager = averager_of(group, head_dim)

    def undo(at):
        def norm_back(g, hat_ref, rstd_ref, gain):
            hat = hat_ref[at, :]
            dgain = jnp.sum(g * hat, axis=0, keepdims=True)
            gy = g * gain
            first = head_mean(gy, averager)
            second = head_mean(gy * hat, averager)
            return rstd_ref[at, :] * (gy - first - hat * second), dgain

        gqn = gq_s[at, :]
        gq, dqg = norm_back(gqn, qhat_ref, qrstd_ref, qg_ref[...])
        norm_ref[0:1, :] += factor * dqg
        norm_ref[1:2, :] += factor * jnp.sum(gqn, axis=0, keepdims=True)
        gk, dkg = norm_back(gk_s[at, :], khat_ref, krstd_ref, kg_ref[...])
        norm_ref[2:3, :] += factor * dkg
        total = gh1_s[at, :]
        for j, (g, w_ref) in enumerate(((gq, wq_ref), (gk, wk_ref), (gv_s[at, :], wv_ref))):
            g16 = g.astype(BF16)
            g16_s[j, at, :] = g16
            total += dot(g16, w_ref[...], NT)
        gh1_s[at, :] = total

    row_loop(rows, chunk, undo)
    for j in range(3):
        g16 = g16_s[j]
        dw_ref[j] = factor * dot(h1t_s[...], g16)
        db_ref[j] = factor * jnp.sum(g16.astype(F32), axis=0, keepdims=True)

    @pl.when(step == last)
    def _():
        def finish(at):
            hat, rstd = row_stats(x_ref[at, :].astype(F32))
            gy = gh1_s[at, :]
            small_ref[0:1, :] += factor * jnp.sum(gy * hat, axis=0, keepdims=True)
            small_ref[1:2, :] += factor * jnp.sum(gy, axis=0, keepdims=True)
            gy = gy * g1_ref[...]
            first = jnp.mean(gy, axis=-1, keepdims=True)
            second = jnp.mean(gy * hat, axis=-1, keepdims=True)
            gx_ref[at, :] = (gr_ref[at, :] + rstd * (gy - first - hat * second)).astype(BF16)

        row_loop(rows, chunk // 2, finish)


def shape(dims, dtype):
    return jax.ShapeDtypeStruct(dims, dtype)


def whole(dims):
    return pl.BlockSpec(dims, lambda i: (0,) * len(dims))


def columns(rows, width, skip=0):
    return pl.BlockSpec((rows, width), lambda i: (0, i + skip))


SMEM = pl.BlockSpec(memory_space=pltpu.SMEM)
PARAMS = pltpu.CompilerParams(vmem_limit_bytes=VMEM)


def layer(
    tokens, ln1_gain, ln1_bias, w_qkv, b_qkv, qnorm_gain, qnorm_bias, knorm_gain, w_out, b_out,
    ln2_gain, ln2_bias, w_up, b_up, w_down, b_down, segment_ids, bucket_ids, share_counts, cotangent,
):
    rows, width = tokens.shape
    head_dim = qnorm_gain.shape[0]
    hidden = w_up.shape[1]
    blocks = 2
    span = rows // blocks
    group = min(GROUP, width)
    steps = width // group
    heads = group // head_dim

    def row(v):
        return v.astype(F32).reshape(1, -1)

    def tiled(v):
        return jnp.tile(row(v), (1, heads))

    counts = share_counts.astype(F32)
    share = jnp.sum(jnp.where(jnp.arange(2) == bucket_ids[0], counts, 0.0)) / jnp.sum(counts)
    total_slots = lax.axis_size("wide") * lax.axis_size("narrow") * rows
    factor = (share * lax.rsqrt(jnp.float32(total_slots))).reshape(1)
    segc = segment_ids.reshape(rows, 1)
    segr = segment_ids.reshape(blocks, 1, span)
    live = (segc >= 0).astype(F32)
    bias_qkv = row(b_qkv)
    q_gain, q_bias, k_gain = tiled(qnorm_gain), tiled(qnorm_bias), tiled(knorm_gain)

    by_group = columns(rows, group)
    lse_spec = pl.BlockSpec((heads, blocks, 1, span), lambda i: (i, 0, 0, 0))
    h1, qn, kn, v16, qhat, khat, qrstd, krstd, lse, o_t, resid, h2 = pl.pallas_call(
        functools.partial(forward_kernel, head_dim, blocks),
        grid=(steps,),
        in_specs=[
            SMEM,
            whole((rows, width)),
            whole((1, width)),
            whole((1, width)),
            columns(width, group),
            columns(width, group, steps),
            columns(width, group, 2 * steps),
            columns(1, group),
            columns(1, group, steps),
            columns(1, group, 2 * steps),
            whole((1, group)),
            whole((1, group)),
            whole((1, group)),
            pl.BlockSpec((group, width), lambda i: (i, 0)),
            whole((1, width)),
            whole((1, width)),
            whole((1, width)),
            whole((rows, 1)),
            whole((blocks, 1, span)),
        ],
        out_specs=[
            whole((rows, width)),
            by_group,
            by_group,
            by_group,
            by_group,
            by_group,
            by_group,
            by_group,
            lse_spec,
            pl.BlockSpec((blocks, group, span), lambda i: (0, i, 0)),
            whole((rows, width)),
            whole((rows, width)),
        ],
        out_shape=[
            shape((rows, width), BF16),
            shape((rows, width), BF16),
            shape((rows, width), BF16),
            shape((rows, width), BF16),
            shape((rows, width), F32),
            shape((rows, width), F32),
            shape((rows, width), F32),
            shape((rows, width), F32),
            shape((steps * heads, blocks, 1, span), F32),
            shape((blocks, width, span), BF16),
            shape((rows, width), F32),
            shape((rows, width), BF16),
        ],
        scratch_shapes=[
            pltpu.VMEM((blocks, blocks, span, span), F32),
            pltpu.VMEM((blocks, group, span), BF16),
            pltpu.VMEM((blocks, group, span), F32),
            pltpu.VMEM((rows, group), BF16),
        ],
        compiler_params=PARAMS,
        name="attention_forward",
    )(
        bucket_ids, tokens, row(ln1_gain), row(ln1_bias), w_qkv, w_qkv, w_qkv, bias_qkv, bias_qkv, bias_qkv,
        q_gain, q_bias, k_gain, w_out, row(b_out), row(ln2_gain), row(ln2_bias), segc, segr,
    )

    ff = min(768, hidden)
    out_tokens, grad_resid, go, d_w_down, d_w_up, d_w_out, d_b_up, small_two = pl.pallas_call(
        functools.partial(mlp_kernel, blocks),
        grid=(hidden // ff,),
        in_specs=[
            SMEM,
            whole((rows, width)),
            whole((rows, width)),
            whole((rows, width)),
            whole((rows, 1)),
            columns(width, ff),
            columns(1, ff),
            pl.BlockSpec((ff, width), lambda i: (i, 0)),
            whole((1, width)),
            whole((1, width)),
            whole((width, width)),
            whole((blocks, width, span)),
        ],
        out_specs=[
            whole((rows, width)),
            whole((rows, width)),
            whole((rows, width)),
            pl.BlockSpec((ff, width), lambda i: (i, 0)),
            columns(width, ff),
            whole((width, width)),
            columns(1, ff),
            whole((8, width)),
        ],
        out_shape=[
            shape((rows, width), BF16),
            shape((rows, width), F32),
            shape((rows, width), BF16),
            shape((hidden, width), F32),
            shape((width, hidden), F32),
            shape((width, width), F32),
            shape((1, hidden), F32),
            shape((8, width), F32),
        ],
        scratch_shapes=[
            pltpu.VMEM((rows, width), BF16),
            pltpu.VMEM((width, rows), BF16),
            pltpu.VMEM((rows, ff), BF16),
            pltpu.VMEM((rows, ff), BF16),
            pltpu.VMEM((rows, width), F32),
            pltpu.VMEM((rows, width), F32),
        ],
        compiler_params=PARAMS,
        name="mlp",
    )(
        factor, h2, resid, cotangent, live, w_up, row(b_up), w_down, row(b_down), row(ln2_gain), w_out, o_t,
    )

    grad_tokens, d_qkv, d_b_qkv, small_one, small_norm = pl.pallas_call(
        functools.partial(backward_kernel, head_dim, blocks),
        grid=(steps,),
        in_specs=[
            SMEM,
            whole((rows, width)),
            whole((rows, width)),
            whole((rows, width)),
            whole((1, width)),
            whole((1, group)),
            whole((1, group)),
            whole((rows, 1)),
            whole((blocks, 1, span)),
            by_group,
            by_group,
            by_group,
            by_group,
            by_group,
            by_group,
            by_group,
            by_group,
            lse_spec,
            columns(width, group),
            columns(width, group, steps),
            columns(width, group, 2 * steps),
        ],
        out_specs=[
            whole((rows, width)),
            pl.BlockSpec((3, width, group), lambda i: (0, 0, i)),
            pl.BlockSpec((3, 1, group), lambda i: (0, 0, i)),
            whole((8, width)),
            whole((8, group)),
        ],
        out_shape=[
            shape((rows, width), BF16),
            shape((3, width, width), F32),
            shape((3, 1, width), F32),
            shape((8, width), F32),
            shape((8, group), F32),
        ],
        scratch_shapes=[
            pltpu.VMEM((blocks, span, span), F32),
            pltpu.VMEM((width, rows), BF16),
            pltpu.VMEM((blocks, group, span), BF16),
            pltpu.VMEM((blocks, group, span), F32),
            pltpu.VMEM((rows, group), F32),
            pltpu.VMEM((rows, group), F32),
            pltpu.VMEM((rows, group), F32),
            pltpu.VMEM((3, rows, group), BF16),
            pltpu.VMEM((rows, width), F32),
        ],
        compiler_params=PARAMS,
        name="attention_backward",
    )(
        factor, tokens, h1, grad_resid, row(ln1_gain), q_gain, k_gain, segc, segr, qn, kn, v16, go,
        qhat, khat, qrstd, krstd, lse, w_qkv, w_qkv, w_qkv,
    )
    return out_tokens, grad_tokens, d_w_down, d_w_up, d_w_out, d_qkv, d_b_up, small_two, d_b_qkv, small_one, small_norm


def on_device(*args):
    width = args[0].shape[1]
    head_dim = args[5].shape[0]
    (out_tokens, grad_tokens, d_w_down, d_w_up, d_w_out, d_qkv, d_b_up, small_two, d_b_qkv, small_one, small_norm) = layer(*args)
    both = ("wide", "narrow")
    d_w_down, d_w_up, d_w_out = lax.psum((d_w_down, d_w_up, d_w_out), both)
    small = jnp.concatenate(
        [
            small_one[:2].reshape(-1),
            d_b_qkv.reshape(-1),
            small_norm[:3].reshape(3, -1, head_dim).sum(axis=1).reshape(-1),
            small_two[:4].reshape(-1),
            d_b_up.reshape(-1),
        ]
    )
    d_qkv, small = lax.psum((d_qkv, small), both)
    d_w_qkv = jnp.transpose(d_qkv, (1, 0, 2)).reshape(width, -1)
    sizes = (width, width, 3 * width, head_dim, head_dim, head_dim, width, width, width, width, d_b_up.size)
    parts, at = [], 0
    for size in sizes:
        parts.append(small[at : at + size])
        at += size
    d_g1, d_b1, d_bqkv, d_qg, d_qb, d_kg, d_bd, d_g2, d_b2, d_bo, d_bu = parts
    return (
        out_tokens, grad_tokens, d_g1, d_b1, d_w_qkv, d_bqkv, d_qg, d_qb, d_kg, d_w_out, d_bo,
        d_g2, d_b2, d_w_up, d_bu, d_w_down, d_bd,
    )


def solution(mesh):
    rows = P(("wide", "narrow"), None)
    in_specs = (rows,) + (P(),) * 15 + (P(("wide", "narrow")), P("wide"), P(), rows)
    out_specs = (rows, rows) + (P(),) * 15
    return jax.shard_map(
        on_device, mesh=mesh, in_specs=in_specs, out_specs=out_specs, check_vma=False
    )
```

time: 1170 us -> 717 us (0.61)
  matrix products: 379 us -> 0 us
  Pallas kernels: 0 us -> 199 us
  other arithmetic: 202 us -> 3.32 us
  local copies, waits for them, and re-layouts: 184 us -> 51.8 us
  waiting for transfers between devices: 333 us -> 388 us
  blocking collectives: 45.8 us -> 58.1 us
    dot_general x26 -> x0, matrix products: 379 us -> none  [the longest x4 96.3 us: scores_of(): jnp.einsum('qhd,khd->hqk', q_part, key16, preferred_element_type=jnp.floa...]
    pallas_call x0 -> x3, Pallas kernels: none -> 199 us  [the longest x1 77.3 us: layer(): pl.pallas_call(functools.partial(mlp_kernel, blocks), grid=(hidden // ff,...]
    reduce_sum x21 -> x2, other arithmetic: 90.9 us -> 1.29 us  [the longest x1 1.26 us: layer(): jnp.sum(counts)]
    convert_element_type x17 -> x1, other arithmetic: 75.1 us -> 0.7 us  [layer(): live = (segc >= 0).astype(F32)]
    psum x1, waiting for transfers between devices: 333 us -> 388 us  [on_device(): d_qkv, small = lax.psum((d_qkv, small), both)]
    unnamed x147 -> x20, local copies, waits for them, and re-layouts: 50.9 us -> 23.3 us
    reshape x8 -> x14, local copies, waits for them, and re-layouts: 35.9 us -> 12.2 us  [the longest x7 8.86 us: row(): return v.astype(F32).reshape(1, -1)]
    slice x5 -> x7, local copies, waits for them, and re-layouts: 21.2 us -> 3.29 us  [the longest x4 2.54 us: on_device(): parts.append(small[at:at + size])]
  transfers between devices with their start and end apart: 1 -> 1, of which waited for: 1 -> 1; matrix products, arithmetic and copies ran while one was open for 5% -> 1% of each run, Pallas kernels for 0% -> 0%
where the time goes in v1:
time: 717 us; the launch traced here: 716 us
  waiting for transfers between devices  388 us (54%)
  Pallas kernels  199 us (28%)
  blocking collectives  58.1 us (8%)
  local copies, waits for them, and re-layouts  51.8 us (7%)
  between operations  16.1 us (2%)
    psum x1, waiting for transfers between devices, on_device(): d_qkv, small = lax.psum((d_qkv, small), both)  388 us
    pallas_call x1, Pallas kernels, layer(): pl.pallas_call(functools.partial(mlp_kernel, blocks), grid=(hidden // ff,...  77.3 us
    pallas_call x1, Pallas kernels, layer(): pl.pallas_call(functools.partial(backward_kernel, head_dim, blocks), grid...  68.1 us
    psum x1, blocking collectives, on_device(): d_qkv, small = lax.psum((d_qkv, small), both)  58.1 us
    pallas_call x1, Pallas kernels, layer(): pl.pallas_call(functools.partial(forward_kernel, head_dim, blocks), grid=...  53.5 us
    unnamed x20, local copies, waits for them, and re-layouts  23.3 us
  transfers between devices with their start and end apart: 1, of which 1 were waited for; matrix products, arithmetic and copies ran while one was open for 1% of the time, Pallas kernels for 0%

profile of v1, /device:TPU:0, one launch (start us, length us, event | category | flops | bytes accessed | tf_op | source)
XLA Modules:
  0.0 715.7 jit_solution(14516045856100180453)
XLA Ops:
  7.2 0.0 all-reduce.3.cloned.1.call-start
  7.2 1.4 reshape.141.segr_ref
  8.6 0.7 compare_convert_fusion
  9.3 1.7 reshape.170.segc_ref
  11.7 0.7 tile.24
  12.3 0.6 tile.25.qg_ref
  13.0 0.7 tile.26
  13.6 0.6 tile.27.qb_ref
  14.3 0.7 tile.28
  14.9 0.6 tile.29.kg_ref
  15.6 1.3 reshape.154.g1_ref
  16.8 1.3 reshape.162.g2_ref
  18.1 1.3 reshape.156.b1_ref
  19.4 1.3 reshape.160.bo_ref
  20.6 1.3 reshape.164.b2_ref
  21.9 1.3 reshape.169.bd_ref
  23.1 1.3 reshape.158.bq_ref.bk_ref.bv_ref
  24.4 1.3 reshape.166
  25.7 1.1 reshape.171.live_ref
  26.8 1.3 convert_reduce_fusion
  29.4 53.5 %attention_forward.1 = (bf16[1152,768]{1,0:T(8,128)(2,1)}, bf16[1152,768]{1,0:T(8,128)(2,1)}, bf16[1152,768]{1,0:T(8,128)(2,1)}, bf16[1152,768]{1,0:T(8,128)(2,1...) custom-call(s32[1]{0:T(128)} %copy.46.bucket_ref, ...), custom_call_target="tpu_custom_call" | custom-call | tf_op jit(solution)/shard_map/attention_forward/pallas_call | solution.py:502
  82.9 77.3 %mlp.1 = (bf16[1152,768]{1,0:T(8,128)(2,1)}, f32[1152,768]{1,0:T(8,128)}, bf16[1152,768]{1,0:T(8,128)(2,1)}, f32[3072,768]{1,0:T(8,128)}, f32[768,3072]{1,0:T(8,...) custom-call(f32[1]{0:T(128)} %bitcast.1.factor_ref, bf16[1152,768]{1,0:T(8,128)(2,1)} %get-tuple-element.42.h2_ref, ...), custom_call_target="tpu_custom_call" | custom-call | tf_op jit(solution)/shard_map/mlp/pallas_call | solution.py:568
  160.2 68.1 %attention_backward.1 = (bf16[1152,768]{1,0:T(8,128)(2,1)}, f32[3,768,768]{2,1,0:T(8,128)}, f32[3,1,768]{2,1,0:T(1,128)}, f32[8,768]{1,0:T(8,128)}, f32[8,256]{1,0:T(8,128)}) custom-call(f32[1]{0:T(128)} %bitcast.1.factor_ref, bf16[1152,768]{1,0:T(8,128)(2,1)} %x_ref.3, bf16[1152,768]{1,0:T(8,128)(2,1)} %get-tuple-element.46.h1_ref, ...), custom_call_target="tpu_custom_call" | custom-call | tf_op jit(solution)/shard_map/attention_backward/pallas_call | solution.py:619
  228.2 8.1 %copy.40 = f32[768,3,768]{0,2,1:T(8,128)} copy(f32[768,3,768]{2,0,1:T(8,128)} %bitcast.10) | data formatting | bytes 14155776 | tf_op jit(solution)/shard_map/transpose | solution.py:695
  236.3 0.0 copy-start.4
  236.3 0.0 all-reduce.3.cloned.1.call-update
  236.3 0.7 copy-done.4
  237.0 0.1 reshape.148
  237.1 0.1 reshape.149
  237.2 0.7 slice.42
  237.9 0.0 copy-done.2
  238.0 0.0 copy-done.3
  238.0 0.0 copy-done.1
  238.0 0.1 concatenate.3
  238.1 58.1 %psum.35 = f32[10176]{0:T(1024)S(1)} all-reduce(f32[10176]{0:T(1024)S(1)} %concatenate.3), channel_id=1, replica_groups=mesh['wide'=8,'narrow'=4] {'wide','narrow'}, use_global_device_ids=true, to_apply=%region_3.4 | all-reduce | flops 10176 | bytes 81408 | tf_op jit(solution)/shard_map/psum | solution.py:694
  296.2 0.6 slice.58
  296.8 0.7 slice.65
  297.5 0.6 fusion.2
  298.1 0.7 fusion.1
  298.8 387.5 %all-reduce.3.cloned.1.call-done = (f32[768,2304]{0,1:T(8,128)}, f32[768,768]{1,0:T(8,128)}, f32[768,3072]{1,0:T(8,128)}, f32[3072,768]{1,0:T(8,128)}) async-done(((f32[768,2304]{0,1:T(8,128)}, f32[768,768]{1,0:T(8,128)}, f32[768,3072]{1,0:T(8,128)}, f32[3072,768]{1,0:T(8,128)}), (f32[768,2304]{0,1:T(8,128)}, f32[768,768]{1,0:T(8,128)}, f32[768,3072]{1,0:T(8,128)}, ...) | async-done | bytes 28311568 | tf_op jit(solution)/shard_map/psum | solution.py:694
  686.3 8.1 %copy.41 = f32[768,2304]{1,0:T(8,128)} copy(f32[768,2304]{0,1:T(8,128)} %get-tuple-element.86) | data formatting | bytes 14155776
  694.4 0.0 copy-done
  694.4 1.4 copy.47
  695.8 9.3 %copy.48 = f32[768,3072]{1,0:T(8,128)} copy(f32[768,3072]{1,0:T(8,128)} %get-tuple-element.112) | data formatting | bytes 18874368
  705.1 0.0 slice-done
  705.1 0.0 slice-done.1
  705.1 0.0 slice-done.2
  705.2 3.7 copy.49
  (15 shorter events, 0.1 us)
Async XLA Ops:
  7.2 679.1 %all-reduce.3.cloned.1.call-start = ((), (), s32[]{:S(2)}) async-start(), calls=%async_computation | async-start | bytes 56623104 | tf_op jit(solution)/shard_map/psum | solution.py:694
  236.3 0.7 copy-start.4
  236.3 1.6 copy-start.2
  236.3 1.7 copy-start.3
  236.3 1.7 copy-start.1
  686.3 8.1 %copy-start = (f32[768,768]{1,0:T(8,128)S(1)}, f32[768,768]{1,0:T(8,128)}, u32[]{:S(2)}) copy-start(f32[768,768]{1,0:T(8,128)} %get-tuple-element.108) | copy-start | bytes 7077892
  694.4 10.7 %slice-start = ((s8[9437184]{0:T(1024)(128)(4,1)}), s8[4194304]{0:T(1024)(128)(4,1)S(1)}, s32[]{:S(2)}) async-start(s8[9437184]{0:T(1024)(128)(4,1)} %bitcast.8), calls=%async_computation.1 | async-start | bytes 8388608
  695.8 9.3 %slice-start.1 = ((s8[9437184]{0:T(1024)(128)(4,1)}), s8[4194304]{0:T(1024)(128)(4,1)S(1)}, s32[]{:S(2)}) async-start(s8[9437184]{0:T(1024)(128)(4,1)} %bitcast.8), calls=%async_computation.2 | async-start | bytes 8388608
  695.8 9.3 %slice-start.2 = ((s8[9437184]{0:T(1024)(128)(4,1)}), s8[1048576]{0:T(1024)(128)(4,1)S(1)}, s32[]{:S(2)}) async-start(s8[9437184]{0:T(1024)(128)(4,1)} %bitcast.8), calls=%async_computation.3 | async-start | bytes 2097152
Sparse Core Ops, SparseCore 0:
  236.5 449.7 all-reduce.2
